TPU v7x, 512 devices: a whole 4x4x16 slice. The times are simulated.
512 devices in a mesh: lat: 16 (over x_hi, y, core), lon: 32 (over z, x_lo).
Axes of the slice: x: 4 (x_hi: 2, x_lo: 2; x = x_hi * 2 + x_lo), y: 4, z: 16, core: 2. Of those that a mesh axis runs over, the one named last changes fastest.
Arguments:
- tokens: bfloat16 [2, 192, 384, 1024], P(None, 'lat', 'lon'), may hold values from -96 to 96
- qkv_weight: bfloat16 [1024, 1536], P('lon'), may hold values from -0.1875 to 0.1875
- out_weight: bfloat16 [512, 1024], P('lon'), may hold values from -1 to 1
- norm_gain: float32 [1024], replicated, may hold values from 0.1 to 1.9
- norm_bias: float32 [1024], replicated, may hold values from -3 to 3
- mixed_grad: bfloat16 [2, 192, 384, 1024], P(None, 'lat', 'lon'), may hold values from -6 to 6
Outputs:
- mixed: bfloat16 [2, 192, 384, 1024], P(None, 'lat', 'lon')
- token_grad: bfloat16 [2, 192, 384, 1024], P(None, 'lat', 'lon')
All inputs are finite; a program needn't handle non-finite values.
Results may differ from a plain program's by a relative error of at most 0.014.
The roundings to bfloat16 on the way count: a program that leaves them out, or rounds other values in their place, can miss the bound.
Values may be sent and summed in bfloat16 or wider, within the bound.
A program may use at most 64 MiB of HBM per device.

v0:
```python
import functools

import jax
import jax.numpy as jnp
from jax import lax
from jax.experimental import pallas as pl
from jax.experimental.pallas import tpu as pltpu
from jax.sharding import PartitionSpec as P

MESH = pl.DeviceIdType.MESH
BF = jnp.bfloat16
F32 = jnp.float32

D = 1024
HEADS = 8
HEAD_DIM = 64
LEV = 2
WIN = 12
INNER = 512
HALF = 6
TOK = LEV * WIN * WIN
QUARTER = TOK // 4
GROUP = 4
GW = GROUP * HEAD_DIM
WIDE = GROUP * TOK
ROWS = 32
EPS = 1e-05

HALVES = ((1, 1), (1, 0), (0, 1), (0, 0))


def nt(a, b):
    return lax.dot_general(a, b, (((1,), (1,)), ((), ())), preferred_element_type=F32)


def nn(a, b):
    return lax.dot_general(a, b, (((1,), (0,)), ((), ())), preferred_element_type=F32)


def tn(a, b):
    return lax.dot_general(a, b, (((0,), (0,)), ((), ())), preferred_element_type=F32)


def ds(start, size):
    return pl.ds(pl.multiple_of(start, size), size)


def kernel(
    n_lat, n_lon,
    t_ref, g_ref, wq_ref, wo_ref, gain_hbm, bias_hbm,
    m_out, d_out,
    wqf, wof, gain_ref, bias_ref, land_t, land_g, xw, gw, packed, heads, attn, agrad, hgrad, pgrad,
    scores, pt, dst, qblk, doblk, wide, mixed, tgrad,
    own_sem, zs, zr, ys, yr, xs, xr, ss, sr, hs, hr,
):
    lat, lon = lax.axis_index("lat"), lax.axis_index("lon")
    nz, ny = n_lon // 2, n_lat // 4
    rq, ro = D // n_lon, INNER // n_lon
    core, par, z = lax.rem(lat, 2), lax.rem(lon, 2), lon // 2
    half, y = lat // (2 * ny), lax.rem(lat // 2, ny)
    lat_lo, lat_hi = lax.rem(lat + n_lat - 1, n_lat), lax.rem(lat + 1, n_lat)
    lon_lo, lon_hi = lax.rem(lon + n_lon - 1, n_lon), lax.rem(lon + 1, n_lon)
    sib = (lat + 1 - 2 * core, lon)
    differ = lax.rem(par + core, 2)
    across = lon + 1 - 2 * par
    x_to = (lax.rem(lat + differ * (n_lat // 2), n_lat), across)
    x_from = (lax.rem(lat + (1 - differ) * (n_lat // 2), n_lat), across)
    west, north, diag = (lat, lon_lo), (lat_lo, lon), (lat_lo, lon_lo)
    east, south, far = (lat, lon_hi), (lat_hi, lon), (lat_hi, lon_hi)

    def offset(yy, e):
        far_pair = e // 2
        size = (1 - far_pair) * (yy + 1) + far_pair * (2 * ny - yy)
        return (1 - 2 * lax.rem(e, 2)) * size

    def z_to(e):
        return (lat, 2 * lax.rem(z + offset(y, e) + nz, nz) + par)

    def source(yy, e):
        return lax.rem(z - offset(yy, e) + nz, nz)

    def exists(yy, e):
        return jnp.logical_or(yy > 0, e < 3)

    def y_to(way):
        return ((half * ny + lax.rem(y + 1 - 2 * way + ny, ny)) * 2 + core, lon)

    def line(group, c):
        return lax.rem(y + ny + (0, 2 * c - 1, 1 - 2 * c, 2)[group], ny)

    barrier = pltpu.get_barrier_semaphore()
    met = [z_to(e) for e in range(4)]
    met += [y_to(0), y_to(1), sib, x_to, x_from, west, north, diag, east, south, far]
    for who in met:
        pl.semaphore_signal(barrier, inc=1, device_id=who, device_id_type=MESH)
    pl.semaphore_wait(barrier, len(met))

    def remote(src, dst, send, recv, who):
        return pltpu.make_async_remote_copy(
            src_ref=src, dst_ref=dst, send_sem=send, recv_sem=recv, device_id=who, device_id_type=MESH
        )

    def quarter(ref, k):
        i, j = HALVES[k]
        return ref.at[pl.ds(i * HALF, HALF), pl.ds(j * HALF, HALF)]

    def halo_in(field, src, land):
        copies = [
            remote(quarter(src, k), land.at[k], hs.at[field * 4 + k], hr.at[field * 4 + k], who)
            for k, who in ((1, west), (2, north), (3, diag))
        ]
        return copies, pltpu.make_async_copy(quarter(src, 0), land.at[0], own_sem.at[4 + field])

    in_t = halo_in(0, t_ref, land_t)
    in_g = halo_in(1, g_ref, land_g)
    def piece(kind, zq, p, c, both=1):
        if kind == 0:
            return wqf.at[pl.ds(pl.multiple_of((zq * 2 + p) * rq, rq), both * rq), ds(c * 768, 768)]
        return wof.at[pl.ds(pl.multiple_of((zq * 2 + p) * ro, ro), both * ro), ds(c * 512, 512)]

    def own_piece(kind):
        return wq_ref.at[:, ds(core * 768, 768)] if kind == 0 else wo_ref.at[:, ds(core * 512, 512)]

    def z_copy(kind, e, zq):
        i = kind * 4 + e
        return remote(own_piece(kind), piece(kind, zq, par, core), zs.at[i], zr.at[i], z_to(e))

    def y_copy(kind, way, e, zq, to):
        ref, i = piece(kind, zq, par, core), (kind * 3 + way) * 4 + e
        return remote(ref, ref, ys.at[i], yr.at[i], y_to(to))

    def x_copy(kind, slot, zq, p):
        ref, i = piece(kind, zq, p, core), kind * 17 + slot
        return remote(ref, ref, xs.at[i], xr.at[i], x_to)

    def x_own(kind):
        i = kind * 17 + 16
        return remote(own_piece(kind), piece(kind, z, par, core), xs.at[i], xr.at[i], x_to)

    def s_copy(kind, slot, zq, c):
        ref, i = piece(kind, zq, 0, c, 2), kind * 17 + slot
        return remote(ref, ref, ss.at[i], sr.at[i], sib)

    def s_own(kind, c):
        ref, i = piece(kind, z, 1 - par, c), kind * 17 + 16
        return remote(ref, ref, ss.at[i], sr.at[i], sib)

    def each(yy, do, waves=(0, 1)):
        def step(e, carry):
            @pl.when(exists(yy, e))
            def _():
                do(e)

            return carry

        lax.fori_loop(2 * waves[0], 2 * waves[-1] + 2, step, 0)

    def begin(kind, waves):
        each(y, lambda e: z_copy(kind, e, z).start(), waves)

    def hop_z(kind, waves, then=None):
        each(y, lambda e: z_copy(kind, e, source(y, e)).wait_recv(), waves)
        if then is not None:
            then()

        def do(e):
            zq = source(y, e)
            y_copy(kind, 0, e, zq, 0).start()
            y_copy(kind, 1, e, zq, 1).start()
            x_copy(kind, e, zq, par).start()

        each(y, do, waves)

    def hop_y(kind, waves):
        def near(e):
            zq = source(line(1, core), e)
            y_copy(kind, core, e, zq, core).wait_recv()
            y_copy(kind, 2, e, zq, core).start()
            x_copy(kind, 4 + e, zq, par).start()

        def other(e):
            zq = source(line(2, core), e)
            y_copy(kind, 1 - core, e, zq, core).wait_recv()
            x_copy(kind, 8 + e, zq, par).start()

        each(line(1, core), near, waves)
        each(line(2, core), other, waves)

    def hop_y2(kind, waves):
        def do(e):
            zq = source(line(3, core), e)
            y_copy(kind, 2, e, zq, core).wait_recv()
            x_copy(kind, 12 + e, zq, par).start()

        each(line(3, core), do, waves)

    def hop_x(kind, waves):
        if waves[0] == 0:
            x_copy(kind, 16, z, 1 - par).wait_recv()
            s_own(kind, core).start()
        for group in range(4):
            def do(e, group=group):
                zq = source(line(group, core), e)
                x_copy(kind, group * 4 + e, zq, 1 - par).wait_recv()
                s_copy(kind, group * 4 + e, zq, core).start()

            each(line(group, core), do, waves)

    def finish(kind):
        s_own(kind, 1 - core).wait_recv()
        for group in range(4):
            def do(e, group=group):
                s_copy(kind, group * 4 + e, source(line(group, 1 - core), e), 1 - core).wait_recv()

            each(line(group, 1 - core), do)

    def all_sent(kind):
        x_own(kind).wait_send()
        s_own(kind, core).wait_send()

        def first(e):
            z_copy(kind, e, z).wait_send()
            y_copy(kind, 0, e, source(y, e), 0).wait_send()
            y_copy(kind, 1, e, source(y, e), 1).wait_send()

        each(y, first)
        each(line(1, core), lambda e: y_copy(kind, 2, e, source(line(1, core), e), core).wait_send())
        for group in range(4):
            def do(e, group=group):
                zq = source(line(group, core), e)
                x_copy(kind, group * 4 + e, zq, par).wait_send()
                s_copy(kind, group * 4 + e, zq, core).wait_send()

            each(line(group, core), do)

    local = [
        pltpu.make_async_copy(wq_ref, wqf.at[ds(lon * rq, rq), :], own_sem.at[0]),
        pltpu.make_async_copy(wo_ref, wof.at[ds(lon * ro, ro), :], own_sem.at[1]),
        pltpu.make_async_copy(gain_hbm, gain_ref, own_sem.at[2]),
        pltpu.make_async_copy(bias_hbm, bias_ref, own_sem.at[3]),
        in_t[1],
        in_g[1],
    ]
    def rows_of(land, field):
        def step(t, carry):
            k, i = 2 * (t // 3), 2 * lax.rem(t, 3)
            two = [land[k + n, pl.ds(i, 2)].reshape(24, D) for n in (0, 1)]
            field[ds(t * 48, 48), :] = jnp.concatenate(two, axis=0)
            return carry

        lax.fori_loop(0, 6, step, 0)

    both = (0, 1)
    begin(0, (0,))
    x_own(0).start()
    for copy in local:
        copy.start()

    def second():
        begin(0, (1,))
        for copy in in_t[0]:
            copy.start()

    hop_z(0, (0,), second)
    hop_y(0, (0,))
    hop_y2(0, (0,))

    def third():
        begin(1, both)
        x_own(1).start()
        for copy in in_g[0]:
            copy.start()

    hop_z(0, (1,), third)
    hop_x(0, (0,))
    hop_y(0, (1,))
    hop_y2(0, (1,))
    for copy in in_t[0]:
        copy.wait_recv()
    for copy in local:
        copy.wait()
    rows_of(land_t, xw)
    hop_x(0, (1,))
    hop_z(1, both)
    for copy in in_g[0]:
        copy.wait_recv()
    rows_of(land_g, gw)
    hop_y(1, both)
    finish(0)

    for n in range(3 * INNER // 256):
        cols = slice(n * 256, n * 256 + 256)
        packed[:, cols] = nn(xw[...], wqf[:, cols]).astype(BF)
    hop_y2(1, both)

    lane_head = lax.broadcasted_iota(jnp.int32, (TOK, GW), 1) // HEAD_DIM
    banned = jnp.where(lat == n_lat - 1, -1e30, 0.0).astype(F32)

    def spread(rows):
        return [rows * (lane_head[0:1] == h).astype(F32).astype(BF) for h in range(GROUP)]

    def columns(g):
        return [ds(n * INNER + g * GW, GW) for n in range(3)]

    def turned(block):
        return block.astype(F32).T.astype(BF)

    def narrow(right, left):
        for c in range(0, WIDE, 384):
            wide[:, c : c + 384] = nn(right, left(slice(c, c + 384)))
        blocks = [wide[h * HEAD_DIM : (h + 1) * HEAD_DIM, h * TOK : (h + 1) * TOK] for h in range(GROUP)]
        return jnp.concatenate(blocks, axis=0).T.astype(BF)

    def forward(g, carry):
        q_at, k_at, v_at = columns(g)
        for h, rows in enumerate(spread(packed[:, q_at])):
            qblk[g, h * TOK : (h + 1) * TOK, :] = rows

        for c in range(0, WIDE, 384):
            scores[:, c : c + 384] = nt(packed[:, k_at], qblk[g, c : c + 384, :])
        for c in range(0, WIDE, 128):
            cols = slice(c, c + 128)
            query = lax.rem(c + lax.broadcasted_iota(jnp.int32, (1, 128), 1), TOK)
            side = (query >= TOK // 2).astype(F32)
            s = jnp.concatenate(
                [scores[: TOK // 2, cols] + side * banned, scores[TOK // 2 :, cols] + (1.0 - side) * banned], axis=0
            )
            top = jnp.max(s, axis=0, keepdims=True)
            e = jnp.exp((s - top) * (HEAD_DIM ** -0.5))
            pt[g, :, cols] = (e * (1.0 / jnp.sum(e, axis=0, keepdims=True))).astype(BF)
        heads[:, q_at] = narrow(turned(packed[:, v_at]), lambda cols: pt[g, :, cols])

        @pl.when(g == 0)
        def _():
            hop_x(1, both)

        return carry

    lax.fori_loop(0, HEADS // GROUP, forward, 0)
    finish(1)

    for n in range(0, D, 256):
        attn[:, n : n + 256] = nn(heads[...], wof[:, n : n + 256]).astype(BF)

    def norm(c, carry):
        rows = ds(c * ROWS, ROWS)
        a = attn[rows, :].astype(F32)
        gain = gain_ref[...]
        scaled = gw[rows, :].astype(F32) * gain
        centered = a - jnp.mean(a, axis=-1, keepdims=True)
        level = scaled - jnp.mean(scaled, axis=-1, keepdims=True)
        inverse = lax.rsqrt(jnp.mean(centered * centered, axis=-1, keepdims=True) + EPS)
        along = jnp.mean(scaled * centered, axis=-1, keepdims=True) * inverse
        normed = centered * inverse
        mixed[rows, :] = (xw[rows, :].astype(F32) + normed * gain + bias_ref[...]).astype(BF)
        agrad[rows, :] = ((level - normed * along) * inverse).astype(BF)
        return carry

    lax.fori_loop(0, TOK // ROWS, norm, 0, unroll=3)

    def halo_out(field, rows, land, out):
        def step(t, carry):
            k, i = 2 * (t // 3), 2 * lax.rem(t, 3)
            block = rows[ds(t * 48, 48), :]
            for n in (0, 1):
                land[k + n, pl.ds(i, 2)] = block[n * 24 : (n + 1) * 24].reshape(2, HALF, LEV, D)
            return carry

        lax.fori_loop(0, 6, step, 0)
        copies = [
            remote(land.at[k], quarter(out, k), hs.at[(field + 2) * 4 + k], hr.at[(field + 2) * 4 + k], who)
            for k, who in ((1, east), (2, south), (3, far))
        ]
        keep = pltpu.make_async_copy(land.at[0], quarter(out, 0), own_sem.at[6 + field])
        for copy in copies:
            copy.start()
        keep.start()
        return copies, keep

    out_m = halo_out(0, mixed, land_t, m_out)

    for n in range(0, INNER, 256):
        hgrad[:, n : n + 256] = nt(agrad[...], wof[n : n + 256, :]).astype(BF)

    def backward(g, carry):
        q_at, k_at, v_at = columns(g)
        for h, rows in enumerate(spread(hgrad[:, q_at])):
            doblk[h * TOK : (h + 1) * TOK, :] = rows

        for c in range(0, WIDE, 384):
            scores[:, c : c + 384] = nt(packed[:, v_at], doblk[c : c + 384, :])
        for c in range(0, WIDE, 128):
            cols = slice(c, c + 128)
            p, dp = pt[g, :, cols].astype(F32), scores[:, cols]
            total = jnp.sum(p * dp, axis=0, keepdims=True)
            dst[:, cols] = (p * (dp - total) * (HEAD_DIM ** -0.5)).astype(BF)
        pgrad[:, q_at] = narrow(turned(packed[:, k_at]), lambda cols: dst[:, cols])
        pgrad[:, v_at] = nn(pt[g], doblk[...]).astype(BF)
        pgrad[:, k_at] = nn(dst[...], qblk[g]).astype(BF)
        return carry

    lax.fori_loop(0, HEADS // GROUP, backward, 0)

    for n in range(0, D, 256):
        cols = slice(n, n + 256)
        sg = nt(pgrad[...], wqf[cols, :]).astype(BF).astype(F32)
        tgrad[:, cols] = (gw[:, cols].astype(F32) + sg).astype(BF)
    out_d = halo_out(1, tgrad, land_g, d_out)

    for kind in (0, 1):
        all_sent(kind)
    for copy in in_t[0] + in_g[0]:
        copy.wait_send()
    for copies, keep in (out_m, out_d):
        keep.wait()
        for copy in copies:
            copy.wait()


def per_device(n_lat, n_lon, tokens, qkv_weight, out_weight, norm_gain, norm_bias, mixed_grad):
    hbm = pl.BlockSpec(memory_space=pltpu.HBM)
    cells = (WIN, WIN, LEV, D)
    m_out, d_out = pl.pallas_call(
        functools.partial(kernel, n_lat, n_lon),
        out_shape=[jax.ShapeDtypeStruct(cells, BF)] * 2,
        in_specs=[hbm] * 6,
        out_specs=[pl.BlockSpec(memory_space=pl.ANY)] * 2,
        scratch_shapes=[
            pltpu.VMEM((D, 3 * INNER), BF),
            pltpu.VMEM((INNER, D), BF),
            pltpu.VMEM((1, D), F32),
            pltpu.VMEM((1, D), F32),
            pltpu.VMEM((4, HALF, HALF, LEV, D), BF),
            pltpu.VMEM((4, HALF, HALF, LEV, D), BF),
            pltpu.VMEM((TOK, D), BF),
            pltpu.VMEM((TOK, D), BF),
            pltpu.VMEM((TOK, 3 * INNER), BF),
            pltpu.VMEM((TOK, INNER), BF),
            pltpu.VMEM((TOK, D), BF),
            pltpu.VMEM((TOK, D), BF),
            pltpu.VMEM((TOK, INNER), BF),
            pltpu.VMEM((TOK, 3 * INNER), BF),
            pltpu.VMEM((TOK, WIDE), F32),
            pltpu.VMEM((2, TOK, WIDE), BF),
            pltpu.VMEM((TOK, WIDE), BF),
            pltpu.VMEM((2, WIDE, GW), BF),
            pltpu.VMEM((WIDE, GW), BF),
            pltpu.VMEM((GW, WIDE), F32),
            pltpu.VMEM((TOK, D), BF),
            pltpu.VMEM((TOK, D), BF),
            pltpu.SemaphoreType.DMA((8,)),
            pltpu.SemaphoreType.DMA((8,)),
            pltpu.SemaphoreType.DMA((8,)),
            pltpu.SemaphoreType.DMA((24,)),
            pltpu.SemaphoreType.DMA((24,)),
            pltpu.SemaphoreType.DMA((34,)),
            pltpu.SemaphoreType.DMA((34,)),
            pltpu.SemaphoreType.DMA((34,)),
            pltpu.SemaphoreType.DMA((34,)),
            pltpu.SemaphoreType.DMA((16,)),
            pltpu.SemaphoreType.DMA((16,)),
        ],
        compiler_params=pltpu.CompilerParams(
            collective_id=0, has_side_effects=True, vmem_limit_bytes=63 * 1024 * 1024
        ),
    )(
        tokens.transpose(1, 2, 0, 3), mixed_grad.transpose(1, 2, 0, 3), qkv_weight, out_weight,
        norm_gain.reshape(1, D), norm_bias.reshape(1, D),
    )
    return m_out.transpose(2, 0, 1, 3), d_out.transpose(2, 0, 1, 3)


def solution(mesh):
    placed = (
        P(None, "lat", "lon", None),
        P("lon", None),
        P("lon", None),
        P(),
        P(),
        P(None, "lat", "lon", None),
    )
    return jax.shard_map(
        functools.partial(per_device, mesh.shape["lat"], mesh.shape["lon"]),
        mesh=mesh,
        in_specs=placed,
        out_specs=(P(None, "lat", "lon", None), P(None, "lat", "lon", None)),
        check_vma=False,
    )
```

profile of v0, /device:TPU:1, one launch (start us, length us, event | category | flops | bytes accessed | tf_op | source)
XLA Modules:
  0.0 80.1 jit_solution(10238926668891851870)
XLA Ops:
  0.6 76.2 %shard_map.77 = (bf16[12,12,2,1024]{3,2,1,0:T(2,128)(2,1)}, bf16[12,12,2,1024]{3,2,1,0:T(2,128)(2,1)}) custom-call(bf16[12,12,2,1024]{3,2,1,0:T(2,128)(2,1)} %bitcast.6, bf16[12,12,2,1024]{3,2,1,0:T(2,128)(2,1)} %bitcast.7, bf16[32,1536]{1,0:T(8,128)(2,1)} %wq_ref.1, bf16[16,1024]{1,0:T(8,128)(2,1)} %wo_ref.1, f32[1,1024]{1,0:T(1,128)} %bitcast.10, ...), custom_call_target="tpu_custom_call" | custom-call | tf_op jit(solution)/shard_map/pallas_call | solution.py:423
  76.9 0.0 copy-start
  76.9 2.4 %copy.10 = bf16[2,12,12,1024]{3,0,2,1:T(2,128)(2,1)} copy(bf16[2,12,12,1024]{3,0,2,1:T(2,128)(2,1)} %bitcast.9) | data formatting | bytes 1179648
  79.3 0.0 copy-done
  79.3 0.8 %copy.11 = bf16[2,12,12,1024]{3,0,2,1:T(2,128)(2,1)} copy(bf16[2,12,12,1024]{3,0,2,1:T(2,128)(2,1)S(1)} %bitcast.8) | data formatting | bytes 1179648
Async XLA Ops:
  76.9 2.4 %copy-start = (bf16[12,12,2,1024]{3,2,1,0:T(2,128)(2,1)S(1)}, bf16[12,12,2,1024]{3,2,1,0:T(2,128)(2,1)}, u32[]{:S(2)}) copy-start(bf16[12,12,2,1024]{3,2,1,0:T(2,128)(2,1)} %get-tuple-element.5) | copy-start | bytes 1769476
where the time goes:
time: 80.3 us; the launch traced here: 80.1 us
  Pallas kernels  76.2 us (95%)
  local copies, waits for them, and re-layouts  3.25 us (4%)
    pallas_call x1, Pallas kernels, per_device(): pl.pallas_call(functools.partial(kernel, n_lat, n_lon), out_shape=[jax.Sh...  76.2 us
    unnamed x4, local copies, waits for them, and re-layouts  3.25 us

commit v1 on v0

--- a/solution.py
+++ b/solution.py
@@ -49,7 +49,7 @@
     n_lat, n_lon,
     t_ref, g_ref, wq_ref, wo_ref, gain_hbm, bias_hbm,
     m_out, d_out,
-    wqf, wof, gain_ref, bias_ref, land_t, land_g, xw, gw, packed, heads, attn, agrad, hgrad, pgrad,
+    comb, wqf, wof, gain_ref, bias_ref, land_t, land_g, xw, gw, packed, heads, attn, agrad, hgrad, pgrad,
     scores, pt, dst, qblk, doblk, wide, mixed, tgrad,
     own_sem, zs, zr, ys, yr, xs, xr, ss, sr, hs, hr,
 ):
@@ -79,20 +79,29 @@
     def source(yy, e):
         return lax.rem(z - offset(yy, e) + nz, nz)
 
-    def exists(yy, e):
-        return jnp.logical_or(yy > 0, e < 3)
-
     def y_to(way):
         return ((half * ny + lax.rem(y + 1 - 2 * way + ny, ny)) * 2 + core, lon)
 
     def line(group, c):
         return lax.rem(y + ny + (0, 2 * c - 1, 1 - 2 * c, 2)[group], ny)
+
+    own = [
+        (wq_ref.at[:, 0:D], comb.at[0, par, 0]),
+        (wq_ref.at[:, D:], comb.at[1, par, 0, :, 0:INNER]),
+        (wo_ref.at[:, 0:INNER], comb.at[1, par, 0, 0:ro, INNER:]),
+        (wo_ref.at[:, INNER:], comb.at[1, par, 0, ro:, INNER:]),
+    ]
+    own = [pltpu.make_async_copy(src, to, own_sem.at[8 + k]) for k, (src, to) in enumerate(own)]
+    for copy in own:
+        copy.start()
 
     barrier = pltpu.get_barrier_semaphore()
     met = [z_to(e) for e in range(4)]
     met += [y_to(0), y_to(1), sib, x_to, x_from, west, north, diag, east, south, far]
     for who in met:
         pl.semaphore_signal(barrier, inc=1, device_id=who, device_id_type=MESH)
+    for copy in own:
+        copy.wait()
     pl.semaphore_wait(barrier, len(met))
 
     def remote(src, dst, send, recv, who):
@@ -113,134 +122,54 @@
 
     in_t = halo_in(0, t_ref, land_t)
     in_g = halo_in(1, g_ref, land_g)
-    def piece(kind, zq, p, c, both=1):
-        if kind == 0:
-            return wqf.at[pl.ds(pl.multiple_of((zq * 2 + p) * rq, rq), both * rq), ds(c * 768, 768)]
-        return wof.at[pl.ds(pl.multiple_of((zq * 2 + p) * ro, ro), both * ro), ds(c * 512, 512)]
-
-    def own_piece(kind):
-        return wq_ref.at[:, ds(core * 768, 768)] if kind == 0 else wo_ref.at[:, ds(core * 512, 512)]
-
-    def z_copy(kind, e, zq):
-        i = kind * 4 + e
-        return remote(own_piece(kind), piece(kind, zq, par, core), zs.at[i], zr.at[i], z_to(e))
-
-    def y_copy(kind, way, e, zq, to):
-        ref, i = piece(kind, zq, par, core), (kind * 3 + way) * 4 + e
-        return remote(ref, ref, ys.at[i], yr.at[i], y_to(to))
-
-    def x_copy(kind, slot, zq, p):
-        ref, i = piece(kind, zq, p, core), kind * 17 + slot
+    def slots(wave, group, count=1):
+        return pl.ds(1 + wave * 8 + group * 2, count * 2)
+
+    def z_copy(e):
+        return remote(
+            comb.at[core, par, 0], comb.at[core, par, 1 + e // 2 * 8 + e % 2], zs.at[e], zr.at[e], z_to(e)
+        )
+
+    def y_copy(wave, k):
+        src, dst = ((0, 1), (0, 2), (1, 3))[k]
+        i = wave * 3 + k
+        return remote(
+            comb.at[core, par, slots(wave, src)], comb.at[core, par, slots(wave, dst)], ys.at[i], yr.at[i],
+            y_to(1 - core if k == 1 else core),
+        )
+
+    def x_copy(wave, k, p):
+        ref = comb.at[core, p, slots(wave, (0, 1, 3)[k], (1, 2, 1)[k])] if wave < 2 else comb.at[core, p, 0]
+        i = wave * 3 + k
         return remote(ref, ref, xs.at[i], xr.at[i], x_to)
 
-    def x_own(kind):
-        i = kind * 17 + 16
-        return remote(own_piece(kind), piece(kind, z, par, core), xs.at[i], xr.at[i], x_to)
-
-    def s_copy(kind, slot, zq, c):
-        ref, i = piece(kind, zq, 0, c, 2), kind * 17 + slot
-        return remote(ref, ref, ss.at[i], sr.at[i], sib)
-
-    def s_own(kind, c):
-        ref, i = piece(kind, z, 1 - par, c), kind * 17 + 16
-        return remote(ref, ref, ss.at[i], sr.at[i], sib)
-
-    def each(yy, do, waves=(0, 1)):
-        def step(e, carry):
-            @pl.when(exists(yy, e))
-            def _():
-                do(e)
-
-            return carry
-
-        lax.fori_loop(2 * waves[0], 2 * waves[-1] + 2, step, 0)
-
-    def begin(kind, waves):
-        each(y, lambda e: z_copy(kind, e, z).start(), waves)
-
-    def hop_z(kind, waves, then=None):
-        each(y, lambda e: z_copy(kind, e, source(y, e)).wait_recv(), waves)
-        if then is not None:
-            then()
-
-        def do(e):
-            zq = source(y, e)
-            y_copy(kind, 0, e, zq, 0).start()
-            y_copy(kind, 1, e, zq, 1).start()
-            x_copy(kind, e, zq, par).start()
-
-        each(y, do, waves)
-
-    def hop_y(kind, waves):
-        def near(e):
-            zq = source(line(1, core), e)
-            y_copy(kind, core, e, zq, core).wait_recv()
-            y_copy(kind, 2, e, zq, core).start()
-            x_copy(kind, 4 + e, zq, par).start()
-
-        def other(e):
-            zq = source(line(2, core), e)
-            y_copy(kind, 1 - core, e, zq, core).wait_recv()
-            x_copy(kind, 8 + e, zq, par).start()
-
-        each(line(1, core), near, waves)
-        each(line(2, core), other, waves)
-
-    def hop_y2(kind, waves):
-        def do(e):
-            zq = source(line(3, core), e)
-            y_copy(kind, 2, e, zq, core).wait_recv()
-            x_copy(kind, 12 + e, zq, par).start()
-
-        each(line(3, core), do, waves)
-
-    def hop_x(kind, waves):
-        if waves[0] == 0:
-            x_copy(kind, 16, z, 1 - par).wait_recv()
-            s_own(kind, core).start()
-        for group in range(4):
-            def do(e, group=group):
-                zq = source(line(group, core), e)
-                x_copy(kind, group * 4 + e, zq, 1 - par).wait_recv()
-                s_copy(kind, group * 4 + e, zq, core).start()
-
-            each(line(group, core), do, waves)
-
-    def finish(kind):
-        s_own(kind, 1 - core).wait_recv()
-        for group in range(4):
-            def do(e, group=group):
-                s_copy(kind, group * 4 + e, source(line(group, 1 - core), e), 1 - core).wait_recv()
-
-            each(line(group, 1 - core), do)
-
-    def all_sent(kind):
-        x_own(kind).wait_send()
-        s_own(kind, core).wait_send()
-
-        def first(e):
-            z_copy(kind, e, z).wait_send()
-            y_copy(kind, 0, e, source(y, e), 0).wait_send()
-            y_copy(kind, 1, e, source(y, e), 1).wait_send()
-
-        each(y, first)
-        each(line(1, core), lambda e: y_copy(kind, 2, e, source(line(1, core), e), core).wait_send())
-        for group in range(4):
-            def do(e, group=group):
-                zq = source(line(group, core), e)
-                x_copy(kind, group * 4 + e, zq, par).wait_send()
-                s_copy(kind, group * 4 + e, zq, core).wait_send()
-
-            each(line(group, core), do)
+    def s_copy(wave, c):
+        ref = comb.at[c, :, slots(wave, 0, 4)] if wave < 2 else comb.at[c, 1 - par, 0]
+        return remote(ref, ref, ss.at[wave], sr.at[wave], sib)
+
+    def place(wave):
+        found = [(c, slots(wave, j).start + i, source(line(j, c), 2 * wave + i))
+                 for c in range(2) for j in range(4) for i in range(2)]
+        if wave == 0:
+            found += [(0, 0, z), (1, 0, z)]
+        for c, slot, zq in found:
+            for p in range(2):
+                rows = ds((zq * 2 + p) * rq, rq)
+                if c == 0:
+                    wqf[rows, 0:D] = comb[0, p, slot]
+                else:
+                    out_rows = ds((zq * 2 + p) * ro, ro)
+                    wqf[rows, D:] = comb[1, p, slot, :, 0:INNER]
+                    wof[out_rows, 0:INNER] = comb[1, p, slot, 0:ro, INNER:]
+                    wof[out_rows, INNER:] = comb[1, p, slot, ro:, INNER:]
 
     local = [
-        pltpu.make_async_copy(wq_ref, wqf.at[ds(lon * rq, rq), :], own_sem.at[0]),
-        pltpu.make_async_copy(wo_ref, wof.at[ds(lon * ro, ro), :], own_sem.at[1]),
         pltpu.make_async_copy(gain_hbm, gain_ref, own_sem.at[2]),
         pltpu.make_async_copy(bias_hbm, bias_ref, own_sem.at[3]),
         in_t[1],
         in_g[1],
     ]
+
     def rows_of(land, field):
         def step(t, carry):
             k, i = 2 * (t // 3), 2 * lax.rem(t, 3)
@@ -250,48 +179,67 @@
 
         lax.fori_loop(0, 6, step, 0)
 
-    both = (0, 1)
-    begin(0, (0,))
-    x_own(0).start()
+    z_copies = [z_copy(e) for e in range(4)]
+    for copy in z_copies[:2]:
+        copy.start()
+    x_copy(2, 0, par).start()
     for copy in local:
         copy.start()
 
-    def second():
-        begin(0, (1,))
-        for copy in in_t[0]:
+    def from_z(wave):
+        for copy in z_copies[2 * wave : 2 * wave + 2]:
+            copy.wait_recv()
+        if wave == 0:
+            for copy in z_copies[2:]:
+                copy.start()
+        y_copy(wave, 0).start()
+        y_copy(wave, 1).start()
+        x_copy(wave, 0, par).start()
+        for copy in (in_t, in_g)[wave][0]:
             copy.start()
 
-    hop_z(0, (0,), second)
-    hop_y(0, (0,))
-    hop_y2(0, (0,))
-
-    def third():
-        begin(1, both)
-        x_own(1).start()
-        for copy in in_g[0]:
-            copy.start()
-
-    hop_z(0, (1,), third)
-    hop_x(0, (0,))
-    hop_y(0, (1,))
-    hop_y2(0, (1,))
+    def from_y(wave):
+        y_copy(wave, 0).wait_recv()
+        y_copy(wave, 2).start()
+        y_copy(wave, 1).wait_recv()
+        x_copy(wave, 1, par).start()
+
+    def from_y2(wave):
+        y_copy(wave, 2).wait_recv()
+        x_copy(wave, 2, par).start()
+
+    def from_x(wave):
+        for k in range(3):
+            x_copy(wave, k, 1 - par).wait_recv()
+        s_copy(wave, core).start()
+
+    from_z(0)
+    from_y(0)
+    from_y2(0)
+    from_z(1)
+    x_copy(2, 0, 1 - par).wait_recv()
+    s_copy(2, core).start()
+    from_x(0)
+    from_y(1)
+    from_y2(1)
     for copy in in_t[0]:
         copy.wait_recv()
     for copy in local:
         copy.wait()
     rows_of(land_t, xw)
-    hop_x(0, (1,))
-    hop_z(1, both)
+    s_copy(2, 1 - core).wait_recv()
+    s_copy(0, 1 - core).wait_recv()
+    place(0)
+    from_x(1)
     for copy in in_g[0]:
         copy.wait_recv()
     rows_of(land_g, gw)
-    hop_y(1, both)
-    finish(0)
+    s_copy(1, 1 - core).wait_recv()
+    place(1)
 
     for n in range(3 * INNER // 256):
         cols = slice(n * 256, n * 256 + 256)
         packed[:, cols] = nn(xw[...], wqf[:, cols]).astype(BF)
-    hop_y2(1, both)
 
     lane_head = lax.broadcasted_iota(jnp.int32, (TOK, GW), 1) // HEAD_DIM
     banned = jnp.where(lat == n_lat - 1, -1e30, 0.0).astype(F32)
@@ -330,14 +278,9 @@
             pt[g, :, cols] = (e * (1.0 / jnp.sum(e, axis=0, keepdims=True))).astype(BF)
         heads[:, q_at] = narrow(turned(packed[:, v_at]), lambda cols: pt[g, :, cols])
 
-        @pl.when(g == 0)
-        def _():
-            hop_x(1, both)
-
         return carry
 
     lax.fori_loop(0, HEADS // GROUP, forward, 0)
-    finish(1)
 
     for n in range(0, D, 256):
         attn[:, n : n + 256] = nn(heads[...], wof[:, n : n + 256]).astype(BF)
@@ -407,8 +350,15 @@
         tgrad[:, cols] = (gw[:, cols].astype(F32) + sg).astype(BF)
     out_d = halo_out(1, tgrad, land_g, d_out)
 
-    for kind in (0, 1):
-        all_sent(kind)
+    for copy in z_copies:
+        copy.wait_send()
+    for wave in range(2):
+        for k in range(3):
+            y_copy(wave, k).wait_send()
+            x_copy(wave, k, par).wait_send()
+        s_copy(wave, core).wait_send()
+    x_copy(2, 0, par).wait_send()
+    s_copy(2, core).wait_send()
     for copy in in_t[0] + in_g[0]:
         copy.wait_send()
     for copies, keep in (out_m, out_d):
@@ -426,6 +376,7 @@
         in_specs=[hbm] * 6,
         out_specs=[pl.BlockSpec(memory_space=pl.ANY)] * 2,
         scratch_shapes=[
+            pltpu.VMEM((2, 2, 17, D // n_lon, D), BF),
             pltpu.VMEM((D, 3 * INNER), BF),
             pltpu.VMEM((INNER, D), BF),
             pltpu.VMEM((1, D), F32),
@@ -448,15 +399,15 @@
             pltpu.VMEM((GW, WIDE), F32),
             pltpu.VMEM((TOK, D), BF),
             pltpu.VMEM((TOK, D), BF),
-            pltpu.SemaphoreType.DMA((8,)),
-            pltpu.SemaphoreType.DMA((8,)),
-            pltpu.SemaphoreType.DMA((8,)),
-            pltpu.SemaphoreType.DMA((24,)),
-            pltpu.SemaphoreType.DMA((24,)),
-            pltpu.SemaphoreType.DMA((34,)),
-            pltpu.SemaphoreType.DMA((34,)),
-            pltpu.SemaphoreType.DMA((34,)),
-            pltpu.SemaphoreType.DMA((34,)),
+            pltpu.SemaphoreType.DMA((12,)),
+            pltpu.SemaphoreType.DMA((4,)),
+            pltpu.SemaphoreType.DMA((4,)),
+            pltpu.SemaphoreType.DMA((6,)),
+            pltpu.SemaphoreType.DMA((6,)),
+            pltpu.SemaphoreType.DMA((7,)),
+            pltpu.SemaphoreType.DMA((7,)),
+            pltpu.SemaphoreType.DMA((3,)),
+            pltpu.SemaphoreType.DMA((3,)),
             pltpu.SemaphoreType.DMA((16,)),
             pltpu.SemaphoreType.DMA((16,)),
         ],

time: 80.3 us -> 81.5 us (1.015)
  the two profiles are of different devices: /device:TPU:1 before, /device:TPU:36 now
where the time goes in v1:
time: 81.5 us; the launch traced here: 81.3 us
  Pallas kernels  77.4 us (95%)
  local copies, waits for them, and re-layouts  3.25 us (4%)
    pallas_call x1, Pallas kernels, per_device(): pl.pallas_call(functools.partial(kernel, n_lat, n_lon), out_shape=[jax.Sh...  77.4 us
    unnamed x4, local copies, waits for them, and re-layouts  3.25 us

profile of v1, /device:TPU:36, one launch (start us, length us, event | category | flops | bytes accessed | tf_op | source)
XLA Modules:
  0.0 81.3 jit_solution(4378382452589394419)
XLA Ops:
  0.6 77.4 %shard_map.77 = (bf16[12,12,2,1024]{3,2,1,0:T(2,128)(2,1)}, bf16[12,12,2,1024]{3,2,1,0:T(2,128)(2,1)}) custom-call(bf16[12,12,2,1024]{3,2,1,0:T(2,128)(2,1)} %bitcast.6, bf16[12,12,2,1024]{3,2,1,0:T(2,128)(2,1)} %bitcast.7, bf16[32,1536]{1,0:T(8,128)(2,1)} %wq_ref.1, bf16[16,1024]{1,0:T(8,128)(2,1)} %wo_ref.1, f32[1,1024]{1,0:T(1,128)} %bitcast.10, ...), custom_call_target="tpu_custom_call" | custom-call | tf_op jit(solution)/shard_map/pallas_call | solution.py:373
  78.0 0.0 copy-start
  78.0 2.4 %copy.10 = bf16[2,12,12,1024]{3,0,2,1:T(2,128)(2,1)} copy(bf16[2,12,12,1024]{3,0,2,1:T(2,128)(2,1)} %bitcast.9) | data formatting | bytes 1179648
  80.5 0.0 copy-done
  80.5 0.8 %copy.11 = bf16[2,12,12,1024]{3,0,2,1:T(2,128)(2,1)} copy(bf16[2,12,12,1024]{3,0,2,1:T(2,128)(2,1)S(1)} %bitcast.8) | data formatting | bytes 1179648
Async XLA Ops:
  78.0 2.4 %copy-start = (bf16[12,12,2,1024]{3,2,1,0:T(2,128)(2,1)S(1)}, bf16[12,12,2,1024]{3,2,1,0:T(2,128)(2,1)}, u32[]{:S(2)}) copy-start(bf16[12,12,2,1024]{3,2,1,0:T(2,128)(2,1)} %get-tuple-element.5) | copy-start | bytes 1769476
